TPU v7x, 32 devices: a whole 2x2x4 slice. The times are simulated.
32 devices in a mesh: shot: 8 (over z, y), slab: 4 (over x, core).
Axes of the slice: x: 2, y: 2, z: 4, core: 2. Of those that a mesh axis runs over, the one named last changes fastest.
Arguments:
- forward_state: float32 [8, 9, 32, 32, 128], P('shot', None, 'slab'), may hold values from -6 to 6
- adjoint_state: float32 [8, 9, 32, 32, 128], P('shot', None, 'slab'), may hold values from -6 to 6
- materials: float32 [10, 32, 32, 128], P(None, 'slab', 'shot'), may hold values from 0.1 to 2, as said below
- wavelet: float32 [4], replicated, may hold values from -4 to 4
- encoding: int32 [8, 16], P('shot'), may hold values from 0 to 1
- source_cells: int32 [8, 16], P('shot'), may hold values from 0 to 131071
- receiver_depth: int32 [32, 32], P('slab'), may hold values from 0 to 3
- receiver_data: float32 [8, 4, 32, 32], P('shot', None, 'slab'), may hold values from -6 to 6
Outputs:
- forward_out: float32 [8, 9, 32, 32, 128], P('shot', None, 'slab')
- adjoint_out: float32 [8, 9, 32, 32, 128], P('shot', None, 'slab')
- gradient: float32 [10, 32, 32, 128], P(None, 'slab', 'shot')
Inputs may be any that keep to these rules, and one draw needn't show every extreme that they name: `materials`: row 0 lies in 0.5 to 1; rows 1, 4, 6 in 1 to 2; rows 2, 3, 5 in 0.1 to 0.4; rows 7, 8, 9 in 0.3 to 1.
All inputs are finite; a program needn't handle non-finite values.
Results may differ from a plain program's by a relative error of at most 0.0001.
Values sent between devices are 32-bit elements; how exact they have to be, the bound alone decides.
A program may use at most 64 MiB of HBM per device.

v0:
```python
import functools

import jax
import jax.numpy as jnp
from jax import lax
from jax.experimental import pallas as pl
from jax.experimental.pallas import tpu as pltpu
from jax.sharding import PartitionSpec as P

STEPS = 4
STEP_SIZE = 0.25
VX, VY, VZ, SXX, SYY, SZZ, SYZ, SXZ, SXY = range(9)
PAIRS = [(0, 0), (0, 1), (0, 2), (1, 1), (1, 2), (2, 2), (3, 3), (4, 4), (5, 5)]


def kernel(
    n,
    slabs,
    scale,
    wavelet_in,
    encoding_in,
    cells_in,
    depth_in,
    data_in,
    fwd_in,
    adj_in,
    mats_in,
    F,
    grad_out,
    wavelet,
    encoding,
    cells,
    depth,
    data,
    up_out,
    dn_out,
    up_got,
    dn_got,
    slots,
    mat,
    acc,
    image,
    inj,
    blocks,
    ry,
    rright,
    rleft,
    load_sem,
    halo_send,
    halo_recv,
    ag_recv,
    ag_send_z,
    ag_send_o,
    ag_send_y,
    rs_recv_y,
    rs_send_y,
    rs_recv_r,
    rs_send_r,
    rs_recv_l,
    rs_send_l,
):
    _, comps, xr, ny, nz = fwd_in.shape
    tiles, rows, _ = mats_in.shape
    nc = mat.shape[0]
    yb = ny // n
    group = rows // yb
    L = n // 2
    me = lax.axis_index("shot")
    slab = lax.axis_index("slab")
    lo = lax.rem(me, 2)
    hi = me // 2
    partner = hi * 2 + 1 - lo

    small = [
        pltpu.make_async_copy(src, dst, load_sem.at[3 + i])
        for i, (src, dst) in enumerate(
            [
                (wavelet_in, wavelet),
                (encoding_in, encoding),
                (cells_in, cells),
                (depth_in, depth),
                (data_in, data),
            ]
        )
    ]
    loads = [
        pltpu.make_async_copy(fwd_in.at[0], F.at[0, :, pl.ds(1, xr)], load_sem.at[0]),
        pltpu.make_async_copy(adj_in.at[0], F.at[1, :, pl.ds(1, xr)], load_sem.at[1]),
        pltpu.make_async_copy(mats_in, slots.at[me], load_sem.at[2]),
    ]
    for c in loads + small:
        c.start()
    zero_layer = jnp.zeros((ny, nz), jnp.float32)
    mat[0, 0] = zero_layer
    mat[0, xr + 1] = zero_layer
    for w in range(2):
        F[w, VX, 0] = zero_layer
        F[w, VY, xr + 1] = zero_layer
        F[w, VZ, xr + 1] = zero_layer
        for i in range(3):
            for t in range(STEPS):
                up_got[t, w, i] = zero_layer
                dn_got[t, w, i] = zero_layer

    def shot_id(index):
        return {"shot": index}

    def slab_id(index):
        return {"slab": index}

    MESH = pl.DeviceIdType.MESH
    barrier = pltpu.get_barrier_semaphore()

    def greet(cond, device):
        @pl.when(cond)
        def _():
            pl.semaphore_signal(barrier, inc=1, device_id=device, device_id_type=MESH)

    has_r = hi < L - 1
    has_l = hi > 0
    has_up = slab < slabs - 1
    has_dn = slab > 0
    pl.semaphore_signal(barrier, inc=1, device_id=shot_id(partner), device_id_type=MESH)
    greet(has_r, shot_id(me + 2))
    greet(has_l, shot_id(me - 2))
    greet(has_up, slab_id(slab + 1))
    greet(has_dn, slab_id(slab - 1))
    one = jnp.int32(1)
    nul = jnp.int32(0)
    count = (
        one
        + jnp.where(has_r, one, nul)
        + jnp.where(has_l, one, nul)
        + jnp.where(has_up, one, nul)
        + jnp.where(has_dn, one, nul)
    )
    pl.semaphore_wait(barrier, count)

    def remote(src, dst, ss, rs, device):
        return pltpu.make_async_remote_copy(
            src_ref=src,
            dst_ref=dst,
            send_sem=ss,
            recv_sem=rs,
            device_id=device,
            device_id_type=MESH,
        )

    def when(cond, fn):
        pl.when(cond)(fn)

    def to_partner(block, src):
        return remote(
            src, slots.at[block], ag_send_y.at[block // 2], ag_recv.at[block], shot_id(partner)
        )

    def to_line(block, src, by, sem):
        return remote(src, slots.at[block], sem, ag_recv.at[block], shot_id(me + 2 * by))

    own_r = to_line(me, mats_in, 1, ag_send_z.at[me])
    own_l = to_line(me, mats_in, -1, ag_send_o.at[0])
    own_p = to_partner(me, mats_in)
    when(has_r, own_r.start)
    when(has_l, own_l.start)
    own_p.start()

    def halo(kind, t):
        if kind == 0:
            up_src, up_dst = up_out.at[t], up_got.at[t]
            dn_src, dn_dst = dn_out.at[t], dn_got.at[t]
        elif kind == 1:
            up_src, up_dst = F.at[:, VX, xr], F.at[:, VX, 0]
            dn_src, dn_dst = F.at[:, pl.ds(VY, 2), 1], F.at[:, pl.ds(VY, 2), xr + 1]
        else:
            up_src, up_dst = mat.at[0, xr], mat.at[0, 0]
            dn_src, dn_dst = mat.at[0, 1], mat.at[0, xr + 1]
        up = remote(
            up_src, up_dst, halo_send.at[0, kind, t], halo_recv.at[0, kind, t], slab_id(slab + 1)
        )
        dn = remote(
            dn_src, dn_dst, halo_send.at[1, kind, t], halo_recv.at[1, kind, t], slab_id(slab - 1)
        )
        return up, dn

    def halo_start(kind, t):
        up, dn = halo(kind, t)
        when(has_up, up.start)
        when(has_dn, dn.start)

    def halo_wait(kind, t):
        up, dn = halo(kind, t)
        when(has_dn, up.wait_recv)
        when(has_up, dn.wait_recv)

    def halo_sent(kind, t):
        up, dn = halo(kind, t)
        when(has_up, up.wait_send)
        when(has_dn, dn.wait_send)

    for c in loads + small:
        c.wait()
    halo_start(1, 0)

    lane = lax.broadcasted_iota(jnp.int32, (ny, nz), 1)
    row = lax.broadcasted_iota(jnp.int32, (ny, nz), 0)

    def up_y(a):
        return jnp.where(row == ny - 1, 0.0, pltpu.roll(a, ny - 1, 0)) - a

    def down_y(a):
        return a - jnp.where(row == 0, 0.0, pltpu.roll(a, 1, 0))

    def up_z(a):
        return jnp.where(lane == nz - 1, 0.0, pltpu.roll(a, nz - 1, 1)) - a

    def down_z(a):
        return a - jnp.where(lane == 0, 0.0, pltpu.roll(a, 1, 1))

    def pack(t):
        for w in range(2):
            sxy, sxz = F[w, SXY, xr], F[w, SXZ, xr]
            up_out[t, w, 0] = down_y(sxy) + down_z(sxz) - F[w, SXX, xr]
            up_out[t, w, 1] = sxz
            up_out[t, w, 2] = sxy
            syz = F[w, SYZ, 1]
            dn_out[t, w, 0] = F[w, SXY, 1] + up_y(F[w, SYY, 1]) + down_z(syz)
            dn_out[t, w, 1] = F[w, SXZ, 1] + down_y(syz) + up_z(F[w, SZZ, 1])
            dn_out[t, w, 2] = F[w, SXX, 1]
        halo_start(0, t)

    def unpack(t):
        halo_wait(0, t)
        for w in range(2):
            F[w, SXZ, 0] = up_got[t, w, 1]
            F[w, SXY, 0] = up_got[t, w, 2]
            F[w, SXX, xr + 1] = dn_got[t, w, 2]

    def ghosts(t):
        for w in range(2):
            F[w, VX, 0] += mat[0, 0] * (F[w, SXX, 1] + up_got[t, w, 0])
            F[w, VY, xr + 1] += mat[0, xr + 1] * (dn_got[t, w, 0] - F[w, SXY, xr])
            F[w, VZ, xr + 1] += mat[0, xr + 1] * (dn_got[t, w, 1] - F[w, SXZ, xr])

    pack(0)

    eye = lax.broadcasted_iota(jnp.int32, (ny, ny), 0) == lax.broadcasted_iota(
        jnp.int32, (ny, ny), 1
    )

    def column(r):
        wide = jnp.broadcast_to(r, (ny, ny))
        return jnp.sum(jnp.where(eye, wide, 0.0), axis=1, keepdims=True)

    def prepare(x, carry):
        cell = ((slab * xr + x) * ny + row) * nz + lane
        total = jnp.zeros((ny, nz), jnp.float32)
        for j in range(cells.shape[1]):
            sign = (2 * encoding[0, j] - 1).astype(jnp.float32)
            total = total + jnp.where(cell == cells[0, j], sign, 0.0)
        image[x] = total
        hit = lane.astype(jnp.float32) == column(depth[pl.ds(x, 1), :].astype(jnp.float32))
        for t in range(STEPS):
            inj[t, x] = jnp.where(hit, column(data[0, t, pl.ds(x, 1), :]), 0.0)
        return carry

    lax.fori_loop(0, xr, prepare, 0)

    for k in range(1, L):
        def right_moving(k=k):
            b = me - 2 * k
            ref = slots.at[b]
            to_line(b, ref, 1, ag_send_z.at[b]).wait_recv()
            when(has_r, to_line(b, ref, 1, ag_send_z.at[b]).start)
            to_partner(b, ref).start()

        def left_moving(k=k):
            b = me + 2 * k
            ref = slots.at[b]
            to_line(b, ref, -1, ag_send_z.at[b]).wait_recv()
            when(has_l, to_line(b, ref, -1, ag_send_z.at[b]).start)
            to_partner(b, ref).start()

        when(hi >= k, right_moving)
        when(hi + k < L, left_moving)
    for h in range(L):
        b = h * 2 + 1 - lo
        to_partner(b, slots.at[b]).wait_recv()

    def assemble(xg, carry):
        for c in range(nc):
            held = [slots[i, c * (xr // group) + xg] for i in range(n)]
            for j in range(group):
                whole = jnp.concatenate([h[j * yb : (j + 1) * yb] for h in held], axis=0)
                mat[c, xg * group + j + 1] = whole * STEP_SIZE
        return carry

    lax.fori_loop(0, xr // group, assemble, 0)
    halo_start(2, 0)

    def velocity_layer(t, x):
        forces = []
        old = []
        for w in range(2):
            sxx, sxy, sxz = F[w, SXX, x], F[w, SXY, x], F[w, SXZ, x]
            syz = F[w, SYZ, x]
            fx = (F[w, SXX, x + 1] - sxx) + down_y(sxy) + down_z(sxz)
            fy = (sxy - F[w, SXY, x - 1]) + up_y(F[w, SYY, x]) + down_z(syz)
            fz = (sxz - F[w, SXZ, x - 1]) + down_y(syz) + up_z(F[w, SZZ, x])
            forces.append([fx, fy, fz])
            old.append([F[w, VX, x], F[w, VY, x], F[w, VZ, x]])
        term = (
            forces[0][0] * old[1][0] + forces[0][1] * old[1][1] + forces[0][2] * old[1][2]
        )
        acc[0, x] = term if t == 0 else acc[0, x] + term
        buoy = mat[0, x]
        for w in range(2):
            for c in range(3):
                F[w, c, x] = old[w][c] + buoy * forces[w][c]

    def strain_of(w, x):
        vx, vy, vz = F[w, VX, x], F[w, VY, x], F[w, VZ, x]
        return [
            vx - F[w, VX, x - 1],
            down_y(vy),
            down_z(vz),
            up_z(vy) + up_y(vz),
            up_z(vx) + (F[w, VZ, x + 1] - vz),
            up_y(vx) + (F[w, VY, x + 1] - vy),
        ]

    def add_terms(t, x, f, a):
        for i, (p, q) in enumerate(PAIRS):
            term = f[p] * a[q]
            if p != q:
                term = term + f[q] * a[p]
            if t > 0:
                term = term + acc[i + 1, x]
            acc[i + 1, x] = term

    def put_blocks(xg):
        for c in range(nc):
            held = [acc[c, xg * group + j + 1] * scale for j in range(group)]
            for i in range(n):
                blocks[i, c * (xr // group) + xg] = jnp.concatenate(
                    [h[i * yb : (i + 1) * yb] for h in held], axis=0
                )

    def stress_layer(t, x, strains):
        m = [mat[c, x] for c in range(nc)]
        for w in range(2):
            exx, eyy, ezz, gyz, gxz, gxy = strains[w]
            F[w, SXX, x] = F[w, SXX, x] + (m[1] * exx + m[2] * eyy + m[3] * ezz)
            F[w, SYY, x] = F[w, SYY, x] + (m[2] * exx + m[4] * eyy + m[5] * ezz)
            extra = wavelet[t] * image[x - 1] if w == 0 else inj[t, x - 1]
            F[w, SZZ, x] = F[w, SZZ, x] + (m[3] * exx + m[5] * eyy + m[6] * ezz) + extra
            F[w, SYZ, x] = F[w, SYZ, x] + m[7] * gyz
            F[w, SXZ, x] = F[w, SXZ, x] + m[8] * gxz
            F[w, SXY, x] = F[w, SXY, x] + m[9] * gxy

    def over(start, stop, step, fn):
        def one_layer(j, carry):
            fn(start + j * step)
            return carry

        lax.fori_loop(0, (stop - start + step - 1) // step, one_layer, 0)

    def interior(fn):
        over(2, xr, 1, fn)

    def rims(fn):
        over(1, xr + 1, xr - 1, fn)

    for t in range(STEPS):
        last = t == STEPS - 1
        interior(functools.partial(velocity_layer, t))
        unpack(t)
        if t == 0:
            halo_sent(1, 0)
        rims(functools.partial(velocity_layer, t))
        if t == 0:
            halo_wait(1, 0)
            halo_wait(2, 0)
        ghosts(t)

        def both(x, t=t, last=last):
            strains = [strain_of(w, x) for w in range(2)]
            add_terms(t, x, strains[0], strains[1])
            if not last:
                stress_layer(t, x, strains)

        rims(both)
        if not last:
            pack(t + 1)
        interior(both)
    over(0, xr // group, 1, put_blocks)

    def rs_y(d):
        return remote(
            blocks.at[d * 2 + 1 - lo],
            ry.at[d],
            rs_send_y.at[d],
            rs_recv_y.at[d],
            shot_id(partner),
        )

    def rs_r(d):
        return remote(
            ry.at[d], rright.at[d], rs_send_r.at[d], rs_recv_r.at[d], shot_id(me + 2)
        )

    def rs_l(d):
        return remote(ry.at[d], rleft.at[d], rs_send_l.at[d], rs_recv_l.at[d], shot_id(me - 2))

    for k in range(L - 1, 0, -1):
        when(hi + k < L, lambda k=k: rs_y(hi + k).start())
        when(hi >= k, lambda k=k: rs_y(hi - k).start())
    rs_y(hi).start()

    over(1, xr + 1, 1, lambda x: stress_layer(STEPS - 1, x, [strain_of(w, x) for w in range(2)]))

    def add_into(d, extra, target):
        def one_layer(x, carry):
            for c in range(nc):
                i = x * nc + c
                total = ry[d, i] + blocks[d * 2 + lo, i]
                if extra is not None:
                    total = total + extra[d, i]
                target[i] = total
            return carry

        lax.fori_loop(0, tiles // nc, one_layer, 0)

    for k in range(L - 1, 0, -1):
        def send_right(k=k):
            d = hi + k
            rs_y(d).wait_recv()

            def plus():
                rs_r(d).wait_recv()
                add_into(d, rright, ry.at[d])

            when(has_l, plus)
            when(hi == 0, lambda: add_into(d, None, ry.at[d]))
            rs_r(d).start()

        def send_left(k=k):
            d = hi - k
            rs_y(d).wait_recv()

            def plus():
                rs_l(d).wait_recv()
                add_into(d, rleft, ry.at[d])

            when(has_r, plus)
            when(hi == L - 1, lambda: add_into(d, None, ry.at[d]))
            rs_l(d).start()

        when(hi + k < L, send_right)
        when(hi >= k, send_left)

    rs_y(hi).wait_recv()
    add_into(hi, None, grad_out)

    def take(ref):
        def one_layer(x, carry):
            for c in range(nc):
                i = x * nc + c
                grad_out[i] = grad_out[i] + ref[hi, i]
            return carry

        lax.fori_loop(0, tiles // nc, one_layer, 0)

    def from_left():
        rs_r(hi).wait_recv()
        take(rright)

    def from_right():
        rs_l(hi).wait_recv()
        take(rleft)

    when(has_l, from_left)
    when(has_r, from_right)

    when(has_r, own_r.wait_send)
    when(has_l, own_l.wait_send)
    own_p.wait_send()
    for k in range(1, L):
        def right_sent(k=k):
            b = me - 2 * k
            when(has_r, to_line(b, slots.at[b], 1, ag_send_z.at[b]).wait_send)
            to_partner(b, slots.at[b]).wait_send()

        def left_sent(k=k):
            b = me + 2 * k
            when(has_l, to_line(b, slots.at[b], -1, ag_send_z.at[b]).wait_send)
            to_partner(b, slots.at[b]).wait_send()

        when(hi >= k, right_sent)
        when(hi + k < L, left_sent)
        when(hi + k < L, lambda k=k: rs_y(hi + k).wait_send())
        when(hi >= k, lambda k=k: rs_y(hi - k).wait_send())
        when(hi + k < L, lambda k=k: rs_r(hi + k).wait_send())
        when(hi >= k, lambda k=k: rs_l(hi - k).wait_send())
    rs_y(hi).wait_send()
    for t in range(STEPS):
        halo_sent(0, t)
    halo_sent(2, 0)


def write_out(F, grad, fwd_out, adj_out, grad_out, sem):
    xr = fwd_out.shape[2]
    comps = fwd_out.shape[1]
    half = comps // 2
    copies = [pltpu.make_async_copy(grad, grad_out, sem.at[4])]
    for w, out in ((0, fwd_out), (1, adj_out)):
        for j, (first, count) in enumerate(((0, half), (half, comps - half))):
            copies.append(
                pltpu.make_async_copy(
                    F.at[w, pl.ds(first, count), pl.ds(1, xr)],
                    out.at[0, pl.ds(first, count)],
                    sem.at[2 * w + j],
                )
            )
    for c in copies:
        c.start()
    for c in copies:
        c.wait()


def solution(mesh):
    n = mesh.shape["shot"]
    slabs = mesh.shape["slab"]

    def body(fwd, adj, mats, wavelet, encoding, cells, depth, data):
        shots, comps, xr, ny, nz = fwd.shape
        nc, _, yb, _ = mats.shape
        L = n // 2
        scale = float(shots * n * STEPS) ** (-0.5)
        rows = max(8, yb)
        tiles = nc * xr * yb // rows
        flat = mats.reshape(tiles, rows, nz)
        vmem = pl.BlockSpec(memory_space=pltpu.VMEM)
        hbm = pl.BlockSpec(memory_space=pltpu.HBM)
        any_spec = pl.BlockSpec(memory_space=pl.ANY)
        dma = pltpu.SemaphoreType.DMA
        f32 = jnp.float32
        fields, grad = pl.pallas_call(
            functools.partial(kernel, n, slabs, scale),
            out_shape=(
                pltpu.VMEM((2, comps, xr + 2, ny, nz), f32),
                pltpu.VMEM(flat.shape, f32),
            ),
            in_specs=[any_spec] * 8,
            out_specs=(vmem, vmem),
            scratch_shapes=[
                pltpu.SMEM(wavelet.shape, f32),
                pltpu.SMEM(encoding.shape, jnp.int32),
                pltpu.SMEM(cells.shape, jnp.int32),
                pltpu.VMEM(depth.shape, jnp.int32),
                pltpu.VMEM(data.shape, f32),
                pltpu.VMEM((STEPS, 2, 3, ny, nz), f32),
                pltpu.VMEM((STEPS, 2, 3, ny, nz), f32),
                pltpu.VMEM((STEPS, 2, 3, ny, nz), f32),
                pltpu.VMEM((STEPS, 2, 3, ny, nz), f32),
                pltpu.VMEM((n, tiles, rows, nz), f32),
                pltpu.VMEM((nc, xr + 2, ny, nz), f32),
                pltpu.VMEM((nc, xr + 2, ny, nz), f32),
                pltpu.VMEM((xr, ny, nz), f32),
                pltpu.VMEM((STEPS, xr, ny, nz), f32),
                pltpu.VMEM((n, tiles, rows, nz), f32),
                pltpu.VMEM((L, tiles, rows, nz), f32),
                pltpu.VMEM((L, tiles, rows, nz), f32),
                pltpu.VMEM((L, tiles, rows, nz), f32),
                dma((8,)),
                dma((2, 3, STEPS)),
                dma((2, 3, STEPS)),
                dma((n,)),
                dma((n,)),
                dma((1,)),
                dma((L,)),
                dma((L,)),
                dma((L,)),
                dma((L,)),
                dma((L,)),
                dma((L,)),
                dma((L,)),
            ],
            compiler_params=pltpu.CompilerParams(
                collective_id=0, has_side_effects=True, vmem_limit_bytes=56 * 1024 * 1024
            ),
        )(wavelet, encoding, cells, depth, data, fwd, adj, flat)
        fwd_out, adj_out, grad = pl.pallas_call(
            write_out,
            out_shape=(
                pltpu.HBM(fwd.shape, f32),
                pltpu.HBM(adj.shape, f32),
                pltpu.HBM(flat.shape, f32),
            ),
            in_specs=[vmem, vmem],
            out_specs=(hbm, hbm, hbm),
            scratch_shapes=[dma((5,))],
            compiler_params=pltpu.CompilerParams(vmem_limit_bytes=8 * 1024 * 1024),
        )(fields, grad)
        return fwd_out, adj_out, grad.reshape(mats.shape)

    return jax.shard_map(
        body,
        mesh=mesh,
        in_specs=(
            P("shot", None, "slab", None, None),
            P("shot", None, "slab", None, None),
            P(None, "slab", "shot", None),
            P(),
            P("shot", None),
            P("shot", None),
            P("slab", None),
            P("shot", None, "slab", None),
        ),
        out_specs=(
            P("shot", None, "slab", None, None),
            P("shot", None, "slab", None, None),
            P(None, "slab", "shot", None),
        ),
        check_vma=False,
    )
```

profile of v0, /device:TPU:0, one launch (start us, length us, event | category | flops | bytes accessed | tf_op | source)
XLA Modules:
  0.0 60.1 jit_solution(16389125811176813350)
XLA Ops:
  0.6 58.0 %shard_map.103 = (f32[2,9,10,32,128]{4,3,2,1,0:T(8,128)S(1)}, f32[40,8,128]{2,1,0:T(8,128)S(1)}) custom-call(f32[4]{0:T(128)} %wavelet_in.1, s32[1,16]{1,0:T(1,128)} %encoding_in.1, s32[1,16]{1,0:T(1,128)} %cells_in.1, s32[8,32]{1,0:T(8,128)} %depth_in.1, f32[1,4,8,32]{3,2,1,0:T(8,128)} %data_in.1, f32[1,9,8,32,128]{4,3,2,1,0:T(8,128)} %fwd_in.1, ...), custom_call_target="tpu_custom_call" | custom-call | tf_op jit(solution)/shard_map/pallas_call | solution.py:547
  58.6 1.5 %shard_map.104 = (f32[1,9,8,32,128]{4,3,2,1,0:T(8,128)}, f32[1,9,8,32,128]{4,3,2,1,0:T(8,128)}, f32[40,8,128]{2,1,0:T(8,128)}) custom-call(f32[2,9,10,32,128]{4,3,2,1,0:T(8,128)S(1)} %get-tuple-element.8.F, f32[40,8,128]{2,1,0:T(8,128)S(1)} %get-tuple-element.9.grad), custom_call_target="tpu_custom_call" | custom-call | tf_op jit(solution)/shard_map/pallas_call | solution.py:592
where the time goes:
time: 60.2 us; the launch traced here: 60.1 us
  Pallas kernels  59.4 us (99%)
  between operations  0.64 us (1%)
    pallas_call x1, Pallas kernels, body(): pl.pallas_call(functools.partial(kernel, n, slabs, scale), out_shape=(plt...  58 us
    pallas_call x1, Pallas kernels, body(): pl.pallas_call(write_out, out_shape=(pltpu.HBM(fwd.shape, f32), pltpu.HBM...  1.5 us

commit v1 on v0

v1 whole, which is shorter than its diff:
```python
import functools

import jax
import jax.numpy as jnp
from jax import lax
from jax.experimental import pallas as pl
from jax.experimental.pallas import tpu as pltpu
from jax.sharding import PartitionSpec as P

STEPS = 4
STEP_SIZE = 0.25
VX, VY, VZ, SXX, SYY, SZZ, SYZ, SXZ, SXY = range(9)
PAIRS = [(0, 0), (0, 1), (0, 2), (1, 1), (1, 2), (2, 2), (3, 3), (4, 4), (5, 5)]


def kernel(
    n,
    slabs,
    scale,
    wavelet_in,
    encoding_in,
    cells_in,
    depth_in,
    data_in,
    fwd_in,
    adj_in,
    mats_in,
    F,
    grad_out,
    wavelet,
    encoding,
    cells,
    depth,
    data,
    up_out,
    dn_out,
    up_got,
    dn_got,
    slots,
    mat,
    acc,
    image,
    inj,
    blocks,
    ry,
    rright,
    rleft,
    load_sem,
    halo_send,
    halo_recv,
    ag_recv,
    ag_send_z,
    ag_send_o,
    ag_send_y,
    rs_recv_y,
    rs_send_y,
    rs_recv_r,
    rs_send_r,
    rs_recv_l,
    rs_send_l,
):
    _, comps, xr, ny, nz = fwd_in.shape
    tiles, rows, _ = mats_in.shape
    nc = mat.shape[0]
    yb = ny // n
    group = rows // yb
    nh = F.shape[4]
    half = ny // 2
    first = (0, ny - nh)
    early = nh // yb
    L = n // 2
    me = lax.axis_index("shot")
    slab = lax.axis_index("slab")
    lo = lax.rem(me, 2)
    hi = me // 2
    partner = hi * 2 + 1 - lo

    small = [
        pltpu.make_async_copy(src, dst, load_sem.at[3 + i])
        for i, (src, dst) in enumerate(
            [
                (wavelet_in, wavelet),
                (encoding_in, encoding),
                (cells_in, cells),
                (depth_in, depth),
                (data_in, data),
            ]
        )
    ]
    loads = [
        pltpu.make_async_copy(
            src.at[0, :, :, pl.ds(first[s], nh)],
            F.at[s, w, :, pl.ds(1, xr)],
            load_sem.at[8 + 2 * s + w],
        )
        for s in range(2)
        for w, src in ((0, fwd_in), (1, adj_in))
    ]
    loads.append(pltpu.make_async_copy(mats_in, slots.at[me], load_sem.at[2]))
    for c in loads + small:
        c.start()
    mat[0, 0] = jnp.zeros((ny, nz), jnp.float32)
    mat[0, xr + 1] = jnp.zeros((ny, nz), jnp.float32)
    zero_layer = jnp.zeros((nh, nz), jnp.float32)
    for s in range(2):
        for w in range(2):
            F[s, w, VX, 0] = zero_layer
            F[s, w, VY, xr + 1] = zero_layer
            F[s, w, VZ, xr + 1] = zero_layer
            for i in range(3):
                for t in range(STEPS):
                    up_got[s, t, w, i] = zero_layer
                    dn_got[s, t, w, i] = zero_layer

    def shot_id(index):
        return {"shot": index}

    def slab_id(index):
        return {"slab": index}

    MESH = pl.DeviceIdType.MESH
    barrier = pltpu.get_barrier_semaphore()

    def greet(cond, device):
        @pl.when(cond)
        def _():
            pl.semaphore_signal(barrier, inc=1, device_id=device, device_id_type=MESH)

    has_r = hi < L - 1
    has_l = hi > 0
    has_up = slab < slabs - 1
    has_dn = slab > 0
    pl.semaphore_signal(barrier, inc=1, device_id=shot_id(partner), device_id_type=MESH)
    greet(has_r, shot_id(me + 2))
    greet(has_l, shot_id(me - 2))
    greet(has_up, slab_id(slab + 1))
    greet(has_dn, slab_id(slab - 1))
    one = jnp.int32(1)
    nul = jnp.int32(0)
    count = (
        one
        + jnp.where(has_r, one, nul)
        + jnp.where(has_l, one, nul)
        + jnp.where(has_up, one, nul)
        + jnp.where(has_dn, one, nul)
    )
    pl.semaphore_wait(barrier, count)

    def remote(src, dst, ss, rs, device):
        return pltpu.make_async_remote_copy(
            src_ref=src,
            dst_ref=dst,
            send_sem=ss,
            recv_sem=rs,
            device_id=device,
            device_id_type=MESH,
        )

    def when(cond, fn):
        pl.when(cond)(fn)

    def to_partner(block, src):
        return remote(
            src, slots.at[block], ag_send_y.at[block // 2], ag_recv.at[block], shot_id(partner)
        )

    def to_line(block, src, by, sem):
        return remote(src, slots.at[block], sem, ag_recv.at[block], shot_id(me + 2 * by))

    own_r = to_line(me, mats_in, 1, ag_send_z.at[me])
    own_l = to_line(me, mats_in, -1, ag_send_o.at[0])
    own_p = to_partner(me, mats_in)
    when(has_r, own_r.start)
    when(has_l, own_l.start)
    own_p.start()

    def halo(kind, s, t):
        if kind == 0:
            up_src, up_dst = up_out.at[s, t], up_got.at[s, t]
            dn_src, dn_dst = dn_out.at[s, t], dn_got.at[s, t]
        elif kind == 1:
            up_src, up_dst = F.at[s, :, VX, xr], F.at[s, :, VX, 0]
            dn_src, dn_dst = F.at[s, :, pl.ds(VY, 2), 1], F.at[s, :, pl.ds(VY, 2), xr + 1]
        else:
            part = pl.ds(0, nh) if s == 0 else pl.ds(nh, ny - nh)
            up_src, up_dst = mat.at[0, xr, part], mat.at[0, 0, part]
            dn_src, dn_dst = mat.at[0, 1, part], mat.at[0, xr + 1, part]
        i = s * STEPS + t
        up = remote(
            up_src, up_dst, halo_send.at[0, kind, i], halo_recv.at[0, kind, i], slab_id(slab + 1)
        )
        dn = remote(
            dn_src, dn_dst, halo_send.at[1, kind, i], halo_recv.at[1, kind, i], slab_id(slab - 1)
        )
        return up, dn

    def halo_start(kind, s, t):
        up, dn = halo(kind, s, t)
        when(has_up, up.start)
        when(has_dn, dn.start)

    def halo_wait(kind, s, t):
        up, dn = halo(kind, s, t)
        when(has_dn, up.wait_recv)
        when(has_up, dn.wait_recv)

    def halo_sent(kind, s, t):
        up, dn = halo(kind, s, t)
        when(has_up, up.wait_send)
        when(has_dn, dn.wait_send)

    for c in loads + small:
        c.wait()
    for s in range(2):
        halo_start(1, s, 0)

    lane = lax.broadcasted_iota(jnp.int32, (nh, nz), 1)
    row = lax.broadcasted_iota(jnp.int32, (nh, nz), 0)
    wide_lane = lax.broadcasted_iota(jnp.int32, (ny, nz), 1)
    wide_row = lax.broadcasted_iota(jnp.int32, (ny, nz), 0)

    def up_y(a):
        return jnp.where(row == nh - 1, 0.0, pltpu.roll(a, nh - 1, 0)) - a

    def down_y(a):
        return a - jnp.where(row == 0, 0.0, pltpu.roll(a, 1, 0))

    def up_z(a):
        return jnp.where(lane == nz - 1, 0.0, pltpu.roll(a, nz - 1, 1)) - a

    def down_z(a):
        return a - jnp.where(lane == 0, 0.0, pltpu.roll(a, 1, 1))

    def pack(s, t):
        for w in range(2):
            sxy, sxz = F[s, w, SXY, xr], F[s, w, SXZ, xr]
            up_out[s, t, w, 0] = down_y(sxy) + down_z(sxz) - F[s, w, SXX, xr]
            up_out[s, t, w, 1] = sxz
            up_out[s, t, w, 2] = sxy
            syz = F[s, w, SYZ, 1]
            dn_out[s, t, w, 0] = F[s, w, SXY, 1] + up_y(F[s, w, SYY, 1]) + down_z(syz)
            dn_out[s, t, w, 1] = F[s, w, SXZ, 1] + down_y(syz) + up_z(F[s, w, SZZ, 1])
            dn_out[s, t, w, 2] = F[s, w, SXX, 1]
        halo_start(0, s, t)

    def unpack(s, t):
        halo_wait(0, s, t)
        for w in range(2):
            F[s, w, SXZ, 0] = up_got[s, t, w, 1]
            F[s, w, SXY, 0] = up_got[s, t, w, 2]
            F[s, w, SXX, xr + 1] = dn_got[s, t, w, 2]

    def ghosts(s, t):
        part = pl.ds(first[s], nh)
        for w in range(2):
            F[s, w, VX, 0] += mat[0, 0, part] * (F[s, w, SXX, 1] + up_got[s, t, w, 0])
            F[s, w, VY, xr + 1] += mat[0, xr + 1, part] * (dn_got[s, t, w, 0] - F[s, w, SXY, xr])
            F[s, w, VZ, xr + 1] += mat[0, xr + 1, part] * (dn_got[s, t, w, 1] - F[s, w, SXZ, xr])

    for s in range(2):
        pack(s, 0)

    eye = lax.broadcasted_iota(jnp.int32, (ny, ny), 0) == lax.broadcasted_iota(
        jnp.int32, (ny, ny), 1
    )

    def column(r):
        wide = jnp.broadcast_to(r, (ny, ny))
        return jnp.sum(jnp.where(eye, wide, 0.0), axis=1, keepdims=True)

    def prepare(x, carry):
        cell = ((slab * xr + x) * ny + wide_row) * nz + wide_lane
        total = jnp.zeros((ny, nz), jnp.float32)
        for j in range(cells.shape[1]):
            sign = (2 * encoding[0, j] - 1).astype(jnp.float32)
            total = total + jnp.where(cell == cells[0, j], sign, 0.0)
        image[x] = total
        hit = wide_lane.astype(jnp.float32) == column(depth[pl.ds(x, 1), :].astype(jnp.float32))
        for t in range(STEPS):
            inj[t, x] = jnp.where(hit, column(data[0, t, pl.ds(x, 1), :]), 0.0)
        return carry

    lax.fori_loop(0, xr, prepare, 0)

    def arrived(b, by, more):
        ref = slots.at[b]
        to_line(b, ref, by, ag_send_z.at[b]).wait_recv()
        when(more, to_line(b, ref, by, ag_send_z.at[b]).start)
        to_partner(b, ref).start()

    for k in range(1, L):
        when(hi >= k, lambda k=k: arrived(me - 2 * k, 1, has_r))
        when(hi + k < L - 1, lambda k=k: arrived(me + 2 * k, -1, has_l))

    def from_partner(h):
        b = h * 2 + 1 - lo
        to_partner(b, slots.at[b]).wait_recv()

    early_pairs = -(-early // 2)
    for h in range(early_pairs):
        from_partner(h)

    def assemble(s, xg, carry):
        low, high = ((0, early), (early, n))[s]
        for c in range(nc):
            held = [slots[i, c * (xr // group) + xg] for i in range(low, high)]
            for j in range(group):
                whole = jnp.concatenate([h[j * yb : (j + 1) * yb] for h in held], axis=0)
                mat[c, xg * group + j + 1, pl.ds(low * yb, (high - low) * yb)] = (
                    whole * STEP_SIZE
                )
        return carry

    def last_pair():
        when(hi < L - 1, lambda: arrived((L - 1) * 2 + lo, -1, has_l))

    lax.fori_loop(0, xr // group, functools.partial(assemble, 0), 0)
    halo_start(2, 0, 0)

    def velocity_layer(s, t, x):
        forces = []
        old = []
        for w in range(2):
            sxx, sxy, sxz = F[s, w, SXX, x], F[s, w, SXY, x], F[s, w, SXZ, x]
            syz = F[s, w, SYZ, x]
            fx = (F[s, w, SXX, x + 1] - sxx) + down_y(sxy) + down_z(sxz)
            fy = (sxy - F[s, w, SXY, x - 1]) + up_y(F[s, w, SYY, x]) + down_z(syz)
            fz = (sxz - F[s, w, SXZ, x - 1]) + down_y(syz) + up_z(F[s, w, SZZ, x])
            forces.append([fx, fy, fz])
            old.append([F[s, w, VX, x], F[s, w, VY, x], F[s, w, VZ, x]])
        term = (
            forces[0][0] * old[1][0] + forces[0][1] * old[1][1] + forces[0][2] * old[1][2]
        )
        acc[s, 0, x] = term if t == 0 else acc[s, 0, x] + term
        buoy = mat[0, x, pl.ds(first[s], nh)]
        for w in range(2):
            for c in range(3):
                F[s, w, c, x] = old[w][c] + buoy * forces[w][c]

    def strain_of(s, w, x):
        vx, vy, vz = F[s, w, VX, x], F[s, w, VY, x], F[s, w, VZ, x]
        return [
            vx - F[s, w, VX, x - 1],
            down_y(vy),
            down_z(vz),
            up_z(vy) + up_y(vz),
            up_z(vx) + (F[s, w, VZ, x + 1] - vz),
            up_y(vx) + (F[s, w, VY, x + 1] - vy),
        ]

    def add_terms(s, t, x, f, a):
        for i, (p, q) in enumerate(PAIRS):
            term = f[p] * a[q]
            if p != q:
                term = term + f[q] * a[p]
            if t > 0:
                term = term + acc[s, i + 1, x]
            acc[s, i + 1, x] = term

    def put_blocks(s, xg):
        for c in range(nc):
            held = [acc[s, c, xg * group + j + 1] * scale for j in range(group)]
            for i in range(s * n // 2, (s + 1) * n // 2):
                at = i * yb - first[s]
                blocks[i, c * (xr // group) + xg] = jnp.concatenate(
                    [h[at : at + yb] for h in held], axis=0
                )

    def stress_layer(s, t, x, strains):
        m = [mat[c, x, pl.ds(first[s], nh)] for c in range(nc)]
        for w in range(2):
            exx, eyy, ezz, gyz, gxz, gxy = strains[w]
            F[s, w, SXX, x] = F[s, w, SXX, x] + (m[1] * exx + m[2] * eyy + m[3] * ezz)
            F[s, w, SYY, x] = F[s, w, SYY, x] + (m[2] * exx + m[4] * eyy + m[5] * ezz)
            extra = wavelet[t] * image[x - 1, pl.ds(first[s], nh)] if w == 0 else inj[t, x - 1, pl.ds(first[s], nh)]
            F[s, w, SZZ, x] = F[s, w, SZZ, x] + (m[3] * exx + m[5] * eyy + m[6] * ezz) + extra
            F[s, w, SYZ, x] = F[s, w, SYZ, x] + m[7] * gyz
            F[s, w, SXZ, x] = F[s, w, SXZ, x] + m[8] * gxz
            F[s, w, SXY, x] = F[s, w, SXY, x] + m[9] * gxy

    def over(start, stop, step, fn):
        def one_layer(j, carry):
            fn(start + j * step)
            return carry

        lax.fori_loop(0, (stop - start + step - 1) // step, one_layer, 0)

    def interior(fn):
        over(2, xr, 1, fn)

    def rims(fn):
        over(1, xr + 1, xr - 1, fn)

    def run_step(s, t):
        last = t == STEPS - 1
        interior(functools.partial(velocity_layer, s, t))
        unpack(s, t)
        if t == 0:
            halo_sent(1, s, 0)
        rims(functools.partial(velocity_layer, s, t))
        if t == 0:
            halo_wait(1, s, 0)
            halo_wait(2, s, 0)
        ghosts(s, t)

        def both(x):
            strains = [strain_of(s, w, x) for w in range(2)]
            add_terms(s, t, x, strains[0], strains[1])
            if not last:
                stress_layer(s, t, x, strains)

        rims(both)
        if not last:
            pack(s, t + 1)
        interior(both)
        if last:
            over(0, xr // group, 1, functools.partial(put_blocks, s))

    def last_stress(s):
        over(
            1,
            xr + 1,
            1,
            lambda x: stress_layer(s, STEPS - 1, x, [strain_of(s, w, x) for w in range(2)]),
        )

    def rs_y(d):
        return remote(
            blocks.at[d * 2 + 1 - lo],
            ry.at[d],
            rs_send_y.at[d],
            rs_recv_y.at[d],
            shot_id(partner),
        )

    def rs_r(d):
        return remote(
            ry.at[d], rright.at[d], rs_send_r.at[d], rs_recv_r.at[d], shot_id(me + 2)
        )

    def rs_l(d):
        return remote(ry.at[d], rleft.at[d], rs_send_l.at[d], rs_recv_l.at[d], shot_id(me - 2))

    def inside(s, d):
        return (d >= s * L // 2) & (d < (s + 1) * L // 2)

    def scatter_start(s):
        for k in range(L - 1, 0, -1):
            when(inside(s, hi + k), lambda k=k: rs_y(hi + k).start())
            when(inside(s, hi - k), lambda k=k: rs_y(hi - k).start())
        when(inside(s, hi), lambda: rs_y(hi).start())

    def add_into(d, extra, target):
        def one_layer(x, carry):
            for c in range(nc):
                i = x * nc + c
                total = ry[d, i] + blocks[d * 2 + lo, i]
                if extra is not None:
                    total = total + extra[d, i]
                target[i] = total
            return carry

        lax.fori_loop(0, tiles // nc, one_layer, 0)

    def scatter_round(s, k):
        def send_right():
            d = hi + k
            rs_y(d).wait_recv()

            def plus():
                rs_r(d).wait_recv()
                add_into(d, rright, ry.at[d])

            when(has_l, plus)
            when(hi == 0, lambda: add_into(d, None, ry.at[d]))
            rs_r(d).start()

        def send_left():
            d = hi - k
            rs_y(d).wait_recv()

            def plus():
                rs_l(d).wait_recv()
                add_into(d, rleft, ry.at[d])

            when(has_r, plus)
            when(hi == L - 1, lambda: add_into(d, None, ry.at[d]))
            rs_l(d).start()

        when(inside(s, hi + k), send_right)
        when(inside(s, hi - k), send_left)

    run_step(0, 0)
    last_pair()
    run_step(0, 1)
    run_step(0, 2)
    run_step(0, 3)
    scatter_start(0)
    for h in range(early_pairs, L):
        from_partner(h)
    lax.fori_loop(0, xr // group, functools.partial(assemble, 1), 0)
    halo_start(2, 1, 0)
    last_stress(0)
    rounds = [[] for t in range(STEPS)]
    for k in range(L - 1, 0, -1):
        rounds[min(L - k, STEPS - 1)].append(k)
    for t in range(STEPS):
        run_step(1, t)
        if t == STEPS - 1:
            scatter_start(1)
        for k in rounds[t]:
            scatter_round(0, k)
    last_stress(1)
    for k in range(L - 1, 0, -1):
        scatter_round(1, k)

    rs_y(hi).wait_recv()
    add_into(hi, None, grad_out)

    def take(ref):
        def one_layer(x, carry):
            for c in range(nc):
                i = x * nc + c
                grad_out[i] = grad_out[i] + ref[hi, i]
            return carry

        lax.fori_loop(0, tiles // nc, one_layer, 0)

    def from_left():
        rs_r(hi).wait_recv()
        take(rright)

    def from_right():
        rs_l(hi).wait_recv()
        take(rleft)

    when(has_l, from_left)
    when(has_r, from_right)

    when(has_r, own_r.wait_send)
    when(has_l, own_l.wait_send)
    own_p.wait_send()
    for k in range(1, L):
        def right_sent(k=k):
            b = me - 2 * k
            when(has_r, to_line(b, slots.at[b], 1, ag_send_z.at[b]).wait_send)
            to_partner(b, slots.at[b]).wait_send()

        def left_sent(k=k):
            b = me + 2 * k
            when(has_l, to_line(b, slots.at[b], -1, ag_send_z.at[b]).wait_send)
            to_partner(b, slots.at[b]).wait_send()

        when(hi >= k, right_sent)
        when(hi + k < L, left_sent)
        when(hi + k < L, lambda k=k: rs_y(hi + k).wait_send())
        when(hi >= k, lambda k=k: rs_y(hi - k).wait_send())
        when(hi + k < L, lambda k=k: rs_r(hi + k).wait_send())
        when(hi >= k, lambda k=k: rs_l(hi - k).wait_send())
    rs_y(hi).wait_send()
    for s in range(2):
        for t in range(STEPS):
            halo_sent(0, s, t)
        halo_sent(2, s, 0)


def write_out(F, grad, fwd_out, adj_out, grad_out, sem):
    xr, ny = fwd_out.shape[2:4]
    half = ny // 2
    copies = [pltpu.make_async_copy(grad, grad_out, sem.at[4])]
    for w, out in ((0, fwd_out), (1, adj_out)):
        for s, at in ((0, 0), (1, F.shape[4] - half)):
            copies.append(
                pltpu.make_async_copy(
                    F.at[s, w, :, pl.ds(1, xr), pl.ds(at, half)],
                    out.at[0, :, :, pl.ds(s * half, half)],
                    sem.at[2 * w + s],
                )
            )
    for c in copies:
        c.start()
    for c in copies:
        c.wait()


def solution(mesh):
    n = mesh.shape["shot"]
    slabs = mesh.shape["slab"]

    def body(fwd, adj, mats, wavelet, encoding, cells, depth, data):
        shots, comps, xr, ny, nz = fwd.shape
        nc, _, yb, _ = mats.shape
        L = n // 2
        nh = ny // 2 + 2 * STEPS
        scale = float(shots * n * STEPS) ** (-0.5)
        rows = max(8, yb)
        tiles = nc * xr * yb // rows
        flat = mats.reshape(tiles, rows, nz)
        vmem = pl.BlockSpec(memory_space=pltpu.VMEM)
        hbm = pl.BlockSpec(memory_space=pltpu.HBM)
        any_spec = pl.BlockSpec(memory_space=pl.ANY)
        dma = pltpu.SemaphoreType.DMA
        f32 = jnp.float32
        fields, grad = pl.pallas_call(
            functools.partial(kernel, n, slabs, scale),
            out_shape=(
                pltpu.VMEM((2, 2, comps, xr + 2, nh, nz), f32),
                pltpu.VMEM(flat.shape, f32),
            ),
            in_specs=[any_spec] * 8,
            out_specs=(vmem, vmem),
            scratch_shapes=[
                pltpu.SMEM(wavelet.shape, f32),
                pltpu.SMEM(encoding.shape, jnp.int32),
                pltpu.SMEM(cells.shape, jnp.int32),
                pltpu.VMEM(depth.shape, jnp.int32),
                pltpu.VMEM(data.shape, f32),
                pltpu.VMEM((2, STEPS, 2, 3, nh, nz), f32),
                pltpu.VMEM((2, STEPS, 2, 3, nh, nz), f32),
                pltpu.VMEM((2, STEPS, 2, 3, nh, nz), f32),
                pltpu.VMEM((2, STEPS, 2, 3, nh, nz), f32),
                pltpu.VMEM((n, tiles, rows, nz), f32),
                pltpu.VMEM((nc, xr + 2, ny, nz), f32),
                pltpu.VMEM((2, nc, xr + 2, nh, nz), f32),
                pltpu.VMEM((xr, ny, nz), f32),
                pltpu.VMEM((STEPS, xr, ny, nz), f32),
                pltpu.VMEM((n, tiles, rows, nz), f32),
                pltpu.VMEM((L, tiles, rows, nz), f32),
                pltpu.VMEM((L, tiles, rows, nz), f32),
                pltpu.VMEM((L, tiles, rows, nz), f32),
                dma((12,)),
                dma((2, 3, 2 * STEPS)),
                dma((2, 3, 2 * STEPS)),
                dma((n,)),
                dma((n,)),
                dma((1,)),
                dma((L,)),
                dma((L,)),
                dma((L,)),
                dma((L,)),
                dma((L,)),
                dma((L,)),
                dma((L,)),
            ],
            compiler_params=pltpu.CompilerParams(
                collective_id=0, has_side_effects=True, vmem_limit_bytes=56 * 1024 * 1024
            ),
        )(wavelet, encoding, cells, depth, data, fwd, adj, flat)
        fwd_out, adj_out, grad = pl.pallas_call(
            write_out,
            out_shape=(
                pltpu.HBM(fwd.shape, f32),
                pltpu.HBM(adj.shape, f32),
                pltpu.HBM(flat.shape, f32),
            ),
            in_specs=[vmem, vmem],
            out_specs=(hbm, hbm, hbm),
            scratch_shapes=[dma((5,))],
            compiler_params=pltpu.CompilerParams(vmem_limit_bytes=8 * 1024 * 1024),
        )(fields, grad)
        return fwd_out, adj_out, grad.reshape(mats.shape)

    return jax.shard_map(
        body,
        mesh=mesh,
        in_specs=(
            P("shot", None, "slab", None, None),
            P("shot", None, "slab", None, None),
            P(None, "slab", "shot", None),
            P(),
            P("shot", None),
            P("shot", None),
            P("slab", None),
            P("shot", None, "slab", None),
        ),
        out_specs=(
            P("shot", None, "slab", None, None),
            P("shot", None, "slab", None, None),
            P(None, "slab", "shot", None),
        ),
        check_vma=False,
    )
```

time: 60.2 us -> 72.4 us (1.20)
  the two profiles are of different devices: /device:TPU:0 before, /device:TPU:17 now
where the time goes in v1:
time: 72.4 us; the launch traced here: 72.3 us
  Pallas kernels  71.6 us (99%)
    pallas_call x1, Pallas kernels, body(): pl.pallas_call(functools.partial(kernel, n, slabs, scale), out_shape=(plt...  70.1 us
    pallas_call x1, Pallas kernels, body(): pl.pallas_call(write_out, out_shape=(pltpu.HBM(fwd.shape, f32), pltpu.HBM...  1.5 us

profile of v1, /device:TPU:17, one launch (start us, length us, event | category | flops | bytes accessed | tf_op | source)
XLA Modules:
  0.0 72.3 jit_solution(17420946017079986796)
XLA Ops:
  0.6 70.1 %shard_map.103 = (f32[2,2,9,10,24,128]{5,4,3,2,1,0:T(8,128)S(1)}, f32[40,8,128]{2,1,0:T(8,128)S(1)}) custom-call(f32[4]{0:T(128)} %wavelet_in.1, s32[1,16]{1,0:T(1,128)} %encoding_in.1, s32[1,16]{1,0:T(1,128)} %cells_in.1, s32[8,32]{1,0:T(8,128)} %depth_in.1, f32[1,4,8,32]{3,2,1,0:T(8,128)} %data_in.1, f32[1,9,8,32,128]{4,3,2,1,0:T(8,128)} %fwd_in.1, ...), custom_call_target="tpu_custom_call" | custom-call | tf_op jit(solution)/shard_map/pallas_call | solution.py:604
  70.8 1.5 %shard_map.104 = (f32[1,9,8,32,128]{4,3,2,1,0:T(8,128)}, f32[1,9,8,32,128]{4,3,2,1,0:T(8,128)}, f32[40,8,128]{2,1,0:T(8,128)}) custom-call(f32[2,2,9,10,24,128]{5,4,3,2,1,0:T(8,128)S(1)} %get-tuple-element.8.F, f32[40,8,128]{2,1,0:T(8,128)S(1)} %get-tuple-element.9.grad), custom_call_target="tpu_custom_call" | custom-call | tf_op jit(solution)/shard_map/pallas_call | solution.py:649

commit v2 on v0

--- a/solution.py
+++ b/solution.py
@@ -9,6 +9,7 @@
 
 STEPS = 4
 STEP_SIZE = 0.25
+PAD = 8
 VX, VY, VZ, SXX, SYY, SZZ, SYZ, SXZ, SXY = range(9)
 PAIRS = [(0, 0), (0, 1), (0, 2), (1, 1), (1, 2), (2, 2), (3, 3), (4, 4), (5, 5)]
 
@@ -84,19 +85,31 @@
         )
     ]
     loads = [
-        pltpu.make_async_copy(fwd_in.at[0], F.at[0, :, pl.ds(1, xr)], load_sem.at[0]),
-        pltpu.make_async_copy(adj_in.at[0], F.at[1, :, pl.ds(1, xr)], load_sem.at[1]),
+        pltpu.make_async_copy(fwd_in.at[0], F.at[0, :, pl.ds(1, xr), pl.ds(PAD, ny)], load_sem.at[0]),
+        pltpu.make_async_copy(adj_in.at[0], F.at[1, :, pl.ds(1, xr), pl.ds(PAD, ny)], load_sem.at[1]),
         pltpu.make_async_copy(mats_in, slots.at[me], load_sem.at[2]),
     ]
     for c in loads + small:
         c.start()
+
+    def get(w, c, x, by=0):
+        return F[w, c, x, pl.ds(PAD + by, ny)]
+
+    def put(w, c, x, value):
+        F[w, c, x, pl.ds(PAD, ny)] = value
+
     zero_layer = jnp.zeros((ny, nz), jnp.float32)
     mat[0, 0] = zero_layer
     mat[0, xr + 1] = zero_layer
     for w in range(2):
-        F[w, VX, 0] = zero_layer
-        F[w, VY, xr + 1] = zero_layer
-        F[w, VZ, xr + 1] = zero_layer
+        put(w, VX, 0, zero_layer)
+        put(w, VY, xr + 1, zero_layer)
+        put(w, VZ, xr + 1, zero_layer)
+        for x in range(1, xr + 1):
+            for c in (SXY, SYZ, VY):
+                F[w, c, x, pl.ds(0, PAD)] = jnp.zeros((PAD, nz), jnp.float32)
+            for c in (SYY, VX, VZ):
+                F[w, c, x, pl.ds(PAD + ny, PAD)] = jnp.zeros((PAD, nz), jnp.float32)
         for i in range(3):
             for t in range(STEPS):
                 up_got[t, w, i] = zero_layer
@@ -164,13 +177,16 @@
     when(has_l, own_l.start)
     own_p.start()
 
+    inner = pl.ds(PAD, ny)
+
     def halo(kind, t):
         if kind == 0:
             up_src, up_dst = up_out.at[t], up_got.at[t]
             dn_src, dn_dst = dn_out.at[t], dn_got.at[t]
         elif kind == 1:
-            up_src, up_dst = F.at[:, VX, xr], F.at[:, VX, 0]
-            dn_src, dn_dst = F.at[:, pl.ds(VY, 2), 1], F.at[:, pl.ds(VY, 2), xr + 1]
+            up_src, up_dst = F.at[:, VX, xr, inner], F.at[:, VX, 0, inner]
+            dn_src = F.at[:, pl.ds(VY, 2), 1, inner]
+            dn_dst = F.at[:, pl.ds(VY, 2), xr + 1, inner]
         else:
             up_src, up_dst = mat.at[0, xr], mat.at[0, 0]
             dn_src, dn_dst = mat.at[0, 1], mat.at[0, xr + 1]
@@ -204,11 +220,11 @@
     lane = lax.broadcasted_iota(jnp.int32, (ny, nz), 1)
     row = lax.broadcasted_iota(jnp.int32, (ny, nz), 0)
 
-    def up_y(a):
-        return jnp.where(row == ny - 1, 0.0, pltpu.roll(a, ny - 1, 0)) - a
-
-    def down_y(a):
-        return a - jnp.where(row == 0, 0.0, pltpu.roll(a, 1, 0))
+    def up_y(w, c, x):
+        return get(w, c, x, 1) - get(w, c, x)
+
+    def down_y(w, c, x):
+        return get(w, c, x) - get(w, c, x, -1)
 
     def up_z(a):
         return jnp.where(lane == nz - 1, 0.0, pltpu.roll(a, nz - 1, 1)) - a
@@ -218,28 +234,31 @@
 
     def pack(t):
         for w in range(2):
-            sxy, sxz = F[w, SXY, xr], F[w, SXZ, xr]
-            up_out[t, w, 0] = down_y(sxy) + down_z(sxz) - F[w, SXX, xr]
+            sxz = get(w, SXZ, xr)
+            up_out[t, w, 0] = down_y(w, SXY, xr) + down_z(sxz) - get(w, SXX, xr)
             up_out[t, w, 1] = sxz
-            up_out[t, w, 2] = sxy
-            syz = F[w, SYZ, 1]
-            dn_out[t, w, 0] = F[w, SXY, 1] + up_y(F[w, SYY, 1]) + down_z(syz)
-            dn_out[t, w, 1] = F[w, SXZ, 1] + down_y(syz) + up_z(F[w, SZZ, 1])
-            dn_out[t, w, 2] = F[w, SXX, 1]
+            up_out[t, w, 2] = get(w, SXY, xr)
+            dn_out[t, w, 0] = get(w, SXY, 1) + up_y(w, SYY, 1) + down_z(get(w, SYZ, 1))
+            dn_out[t, w, 1] = get(w, SXZ, 1) + down_y(w, SYZ, 1) + up_z(get(w, SZZ, 1))
+            dn_out[t, w, 2] = get(w, SXX, 1)
         halo_start(0, t)
 
     def unpack(t):
         halo_wait(0, t)
         for w in range(2):
-            F[w, SXZ, 0] = up_got[t, w, 1]
-            F[w, SXY, 0] = up_got[t, w, 2]
-            F[w, SXX, xr + 1] = dn_got[t, w, 2]
+            put(w, SXZ, 0, up_got[t, w, 1])
+            put(w, SXY, 0, up_got[t, w, 2])
+            put(w, SXX, xr + 1, dn_got[t, w, 2])
 
     def ghosts(t):
+        top = xr + 1
         for w in range(2):
-            F[w, VX, 0] += mat[0, 0] * (F[w, SXX, 1] + up_got[t, w, 0])
-            F[w, VY, xr + 1] += mat[0, xr + 1] * (dn_got[t, w, 0] - F[w, SXY, xr])
-            F[w, VZ, xr + 1] += mat[0, xr + 1] * (dn_got[t, w, 1] - F[w, SXZ, xr])
+            fx = get(w, SXX, 1) + up_got[t, w, 0]
+            fy = dn_got[t, w, 0] - get(w, SXY, xr)
+            fz = dn_got[t, w, 1] - get(w, SXZ, xr)
+            put(w, VX, 0, get(w, VX, 0) + mat[0, 0] * fx)
+            put(w, VY, top, get(w, VY, top) + mat[0, top] * fy)
+            put(w, VZ, top, get(w, VZ, top) + mat[0, top] * fz)
 
     pack(0)
 
@@ -301,13 +320,13 @@
         forces = []
         old = []
         for w in range(2):
-            sxx, sxy, sxz = F[w, SXX, x], F[w, SXY, x], F[w, SXZ, x]
-            syz = F[w, SYZ, x]
-            fx = (F[w, SXX, x + 1] - sxx) + down_y(sxy) + down_z(sxz)
-            fy = (sxy - F[w, SXY, x - 1]) + up_y(F[w, SYY, x]) + down_z(syz)
-            fz = (sxz - F[w, SXZ, x - 1]) + down_y(syz) + up_z(F[w, SZZ, x])
+            sxx, sxy, sxz = get(w, SXX, x), get(w, SXY, x), get(w, SXZ, x)
+            syz = get(w, SYZ, x)
+            fx = (get(w, SXX, x + 1) - sxx) + down_y(w, SXY, x) + down_z(sxz)
+            fy = (sxy - get(w, SXY, x - 1)) + up_y(w, SYY, x) + down_z(syz)
+            fz = (sxz - get(w, SXZ, x - 1)) + down_y(w, SYZ, x) + up_z(get(w, SZZ, x))
             forces.append([fx, fy, fz])
-            old.append([F[w, VX, x], F[w, VY, x], F[w, VZ, x]])
+            old.append([get(w, VX, x), get(w, VY, x), get(w, VZ, x)])
         term = (
             forces[0][0] * old[1][0] + forces[0][1] * old[1][1] + forces[0][2] * old[1][2]
         )
@@ -315,17 +334,17 @@
         buoy = mat[0, x]
         for w in range(2):
             for c in range(3):
-                F[w, c, x] = old[w][c] + buoy * forces[w][c]
+                put(w, c, x, old[w][c] + buoy * forces[w][c])
 
     def strain_of(w, x):
-        vx, vy, vz = F[w, VX, x], F[w, VY, x], F[w, VZ, x]
+        vx, vy, vz = get(w, VX, x), get(w, VY, x), get(w, VZ, x)
         return [
-            vx - F[w, VX, x - 1],
-            down_y(vy),
+            vx - get(w, VX, x - 1),
+            down_y(w, VY, x),
             down_z(vz),
-            up_z(vy) + up_y(vz),
-            up_z(vx) + (F[w, VZ, x + 1] - vz),
-            up_y(vx) + (F[w, VY, x + 1] - vy),
+            up_z(vy) + up_y(w, VZ, x),
+            up_z(vx) + (get(w, VZ, x + 1) - vz),
+            up_y(w, VX, x) + (get(w, VY, x + 1) - vy),
         ]
 
     def add_terms(t, x, f, a):
@@ -349,20 +368,23 @@
         m = [mat[c, x] for c in range(nc)]
         for w in range(2):
             exx, eyy, ezz, gyz, gxz, gxy = strains[w]
-            F[w, SXX, x] = F[w, SXX, x] + (m[1] * exx + m[2] * eyy + m[3] * ezz)
-            F[w, SYY, x] = F[w, SYY, x] + (m[2] * exx + m[4] * eyy + m[5] * ezz)
             extra = wavelet[t] * image[x - 1] if w == 0 else inj[t, x - 1]
-            F[w, SZZ, x] = F[w, SZZ, x] + (m[3] * exx + m[5] * eyy + m[6] * ezz) + extra
-            F[w, SYZ, x] = F[w, SYZ, x] + m[7] * gyz
-            F[w, SXZ, x] = F[w, SXZ, x] + m[8] * gxz
-            F[w, SXY, x] = F[w, SXY, x] + m[9] * gxy
+            for c, change in (
+                (SXX, m[1] * exx + m[2] * eyy + m[3] * ezz),
+                (SYY, m[2] * exx + m[4] * eyy + m[5] * ezz),
+                (SZZ, m[3] * exx + m[5] * eyy + m[6] * ezz + extra),
+                (SYZ, m[7] * gyz),
+                (SXZ, m[8] * gxz),
+                (SXY, m[9] * gxy),
+            ):
+                put(w, c, x, get(w, c, x) + change)
 
     def over(start, stop, step, fn):
         def one_layer(j, carry):
             fn(start + j * step)
             return carry
 
-        lax.fori_loop(0, (stop - start + step - 1) // step, one_layer, 0)
+        lax.fori_loop(0, (stop - start + step - 1) // step, one_layer, 0, unroll=2)
 
     def interior(fn):
         over(2, xr, 1, fn)
@@ -508,7 +530,7 @@
 
 
 def write_out(F, grad, fwd_out, adj_out, grad_out, sem):
-    xr = fwd_out.shape[2]
+    xr, ny = fwd_out.shape[2:4]
     comps = fwd_out.shape[1]
     half = comps // 2
     copies = [pltpu.make_async_copy(grad, grad_out, sem.at[4])]
@@ -516,7 +538,7 @@
         for j, (first, count) in enumerate(((0, half), (half, comps - half))):
             copies.append(
                 pltpu.make_async_copy(
-                    F.at[w, pl.ds(first, count), pl.ds(1, xr)],
+                    F.at[w, pl.ds(first, count), pl.ds(1, xr), pl.ds(PAD, ny)],
                     out.at[0, pl.ds(first, count)],
                     sem.at[2 * w + j],
                 )
@@ -547,7 +569,7 @@
         fields, grad = pl.pallas_call(
             functools.partial(kernel, n, slabs, scale),
             out_shape=(
-                pltpu.VMEM((2, comps, xr + 2, ny, nz), f32),
+                pltpu.VMEM((2, comps, xr + 2, ny + 2 * PAD, nz), f32),
                 pltpu.VMEM(flat.shape, f32),
             ),
             in_specs=[any_spec] * 8,

time: 60.2 us -> 58.7 us (0.975)
  Pallas kernels: 59.4 us -> 57.4 us
    pallas_call x1, Pallas kernels: 58 us -> 55.9 us  [body(): pl.pallas_call(functools.partial(kernel, n, slabs, scale), out_shape=(plt...]
where the time goes in v2:
time: 58.7 us; the launch traced here: 58 us
  Pallas kernels  57.4 us (98%)
  between operations  0.64 us (1%)
    pallas_call x1, Pallas kernels, body(): pl.pallas_call(functools.partial(kernel, n, slabs, scale), out_shape=(plt...  55.9 us
    pallas_call x1, Pallas kernels, body(): pl.pallas_call(write_out, out_shape=(pltpu.HBM(fwd.shape, f32), pltpu.HBM...  1.5 us

profile of v2, /device:TPU:0, one launch (start us, length us, event | category | flops | bytes accessed | tf_op | source)
XLA Modules:
  0.0 58.0 jit_solution(14876149398987965863)
XLA Ops:
  0.6 55.9 %shard_map.103 = (f32[2,9,10,48,128]{4,3,2,1,0:T(8,128)S(1)}, f32[40,8,128]{2,1,0:T(8,128)S(1)}) custom-call(f32[4]{0:T(128)} %wavelet_in.1, s32[1,16]{1,0:T(1,128)} %encoding_in.1, s32[1,16]{1,0:T(1,128)} %cells_in.1, s32[8,32]{1,0:T(8,128)} %depth_in.1, f32[1,4,8,32]{3,2,1,0:T(8,128)} %data_in.1, f32[1,9,8,32,128]{4,3,2,1,0:T(8,128)} %fwd_in.1, ...), custom_call_target="tpu_custom_call" | custom-call | tf_op jit(solution)/shard_map/pallas_call | solution.py:569
  56.5 1.5 %shard_map.104 = (f32[1,9,8,32,128]{4,3,2,1,0:T(8,128)}, f32[1,9,8,32,128]{4,3,2,1,0:T(8,128)}, f32[40,8,128]{2,1,0:T(8,128)}) custom-call(f32[2,9,10,48,128]{4,3,2,1,0:T(8,128)S(1)} %get-tuple-element.8.F, f32[40,8,128]{2,1,0:T(8,128)S(1)} %get-tuple-element.9.grad), custom_call_target="tpu_custom_call" | custom-call | tf_op jit(solution)/shard_map/pallas_call | solution.py:614

commit v3 on v2

--- a/solution.py
+++ b/solution.py
@@ -433,10 +433,21 @@
     def rs_l(d):
         return remote(ry.at[d], rleft.at[d], rs_send_l.at[d], rs_recv_l.at[d], shot_id(me - 2))
 
-    for k in range(L - 1, 0, -1):
-        when(hi + k < L, lambda k=k: rs_y(hi + k).start())
-        when(hi >= k, lambda k=k: rs_y(hi - k).start())
-    rs_y(hi).start()
+    events = []
+    seen = nul
+    for k in range(L - 1, -1, -1):
+        for sign in (1, -1) if k > 0 else (1,):
+            d = hi + sign * k
+            valid = (d >= 0) & (d < L)
+            events.append((k, sign, d, valid, seen))
+            seen = seen + jnp.where(valid, one, nul)
+
+    def start_y(wanted, also):
+        for _, _, d, valid, seen in events:
+            when(also & valid & (seen == wanted), lambda d=d: rs_y(d).start())
+
+    start_y(nul, hi >= 0)
+    start_y(one, hi >= 0)
 
     over(1, xr + 1, 1, lambda x: stress_layer(STEPS - 1, x, [strain_of(w, x) for w in range(2)]))
 
@@ -452,33 +463,22 @@
 
         lax.fori_loop(0, tiles // nc, one_layer, 0)
 
-    for k in range(L - 1, 0, -1):
-        def send_right(k=k):
-            d = hi + k
-            rs_y(d).wait_recv()
-
-            def plus():
-                rs_r(d).wait_recv()
-                add_into(d, rright, ry.at[d])
-
-            when(has_l, plus)
-            when(hi == 0, lambda: add_into(d, None, ry.at[d]))
-            rs_r(d).start()
-
-        def send_left(k=k):
-            d = hi - k
-            rs_y(d).wait_recv()
-
-            def plus():
-                rs_l(d).wait_recv()
-                add_into(d, rleft, ry.at[d])
-
-            when(has_r, plus)
-            when(hi == L - 1, lambda: add_into(d, None, ry.at[d]))
-            rs_l(d).start()
-
-        when(hi + k < L, send_right)
-        when(hi >= k, send_left)
+    def send_line(d, sign):
+        copy, held, more = (rs_r, rright, has_l) if sign > 0 else (rs_l, rleft, has_r)
+        rs_y(d).wait_recv()
+
+        def plus():
+            copy(d).wait_recv()
+            add_into(d, held, ry.at[d])
+
+        when(more, plus)
+        when(jnp.logical_not(more), lambda: add_into(d, None, ry.at[d]))
+        copy(d).start()
+
+    for k, sign, d, valid, seen in events:
+        if k > 0:
+            when(valid, functools.partial(send_line, d, sign))
+            start_y(seen + 2, valid)
 
     rs_y(hi).wait_recv()
     add_into(hi, None, grad_out)

time: 58.7 us -> 59.7 us (1.017)
  Pallas kernels: 57.4 us -> 58.5 us
    pallas_call x1, Pallas kernels: 55.9 us -> 57 us  [body(): pl.pallas_call(functools.partial(kernel, n, slabs, scale), out_shape=(plt...]
where the time goes in v3:
time: 59.7 us; the launch traced here: 59.2 us
  Pallas kernels  58.5 us (98%)
  between operations  0.64 us (1%)
    pallas_call x1, Pallas kernels, body(): pl.pallas_call(functools.partial(kernel, n, slabs, scale), out_shape=(plt...  57 us
    pallas_call x1, Pallas kernels, body(): pl.pallas_call(write_out, out_shape=(pltpu.HBM(fwd.shape, f32), pltpu.HBM...  1.5 us

profile of v3, /device:TPU:0, one launch (start us, length us, event | category | flops | bytes accessed | tf_op | source)
XLA Modules:
  0.0 59.2 jit_solution(10269075309585413764)
XLA Ops:
  0.6 57.0 %shard_map.103 = (f32[2,9,10,48,128]{4,3,2,1,0:T(8,128)S(1)}, f32[40,8,128]{2,1,0:T(8,128)S(1)}) custom-call(f32[4]{0:T(128)} %wavelet_in.1, s32[1,16]{1,0:T(1,128)} %encoding_in.1, s32[1,16]{1,0:T(1,128)} %cells_in.1, s32[8,32]{1,0:T(8,128)} %depth_in.1, f32[1,4,8,32]{3,2,1,0:T(8,128)} %data_in.1, f32[1,9,8,32,128]{4,3,2,1,0:T(8,128)} %fwd_in.1, ...), custom_call_target="tpu_custom_call" | custom-call | tf_op jit(solution)/shard_map/pallas_call | solution.py:569
  57.7 1.5 %shard_map.104 = (f32[1,9,8,32,128]{4,3,2,1,0:T(8,128)}, f32[1,9,8,32,128]{4,3,2,1,0:T(8,128)}, f32[40,8,128]{2,1,0:T(8,128)}) custom-call(f32[2,9,10,48,128]{4,3,2,1,0:T(8,128)S(1)} %get-tuple-element.8.F, f32[40,8,128]{2,1,0:T(8,128)S(1)} %get-tuple-element.9.grad), custom_call_target="tpu_custom_call" | custom-call | tf_op jit(solution)/shard_map/pallas_call | solution.py:614

commit v4 on v2

--- a/solution.py
+++ b/solution.py
@@ -173,9 +173,9 @@
     own_r = to_line(me, mats_in, 1, ag_send_z.at[me])
     own_l = to_line(me, mats_in, -1, ag_send_o.at[0])
     own_p = to_partner(me, mats_in)
+    own_p.start()
     when(has_r, own_r.start)
     when(has_l, own_l.start)
-    own_p.start()
 
     inner = pl.ds(PAD, ny)
 
@@ -289,15 +289,15 @@
             b = me - 2 * k
             ref = slots.at[b]
             to_line(b, ref, 1, ag_send_z.at[b]).wait_recv()
+            to_partner(b, ref).start()
             when(has_r, to_line(b, ref, 1, ag_send_z.at[b]).start)
-            to_partner(b, ref).start()
 
         def left_moving(k=k):
             b = me + 2 * k
             ref = slots.at[b]
             to_line(b, ref, -1, ag_send_z.at[b]).wait_recv()
+            to_partner(b, ref).start()
             when(has_l, to_line(b, ref, -1, ag_send_z.at[b]).start)
-            to_partner(b, ref).start()
 
         when(hi >= k, right_moving)
         when(hi + k < L, left_moving)

time: 58.7 us -> 58.8 us (level)
  no operation moved by 1% of the time
where the time goes in v4:
time: 58.8 us; the launch traced here: 58.1 us
  Pallas kernels  57.4 us (98%)
  between operations  0.64 us (1%)
    pallas_call x1, Pallas kernels, body(): pl.pallas_call(functools.partial(kernel, n, slabs, scale), out_shape=(plt...  55.9 us
    pallas_call x1, Pallas kernels, body(): pl.pallas_call(write_out, out_shape=(pltpu.HBM(fwd.shape, f32), pltpu.HBM...  1.5 us

profile of v4, /device:TPU:0, one launch (start us, length us, event | category | flops | bytes accessed | tf_op | source)
XLA Modules:
  0.0 58.1 jit_solution(17658705782507714084)
XLA Ops:
  0.6 55.9 %shard_map.103 = (f32[2,9,10,48,128]{4,3,2,1,0:T(8,128)S(1)}, f32[40,8,128]{2,1,0:T(8,128)S(1)}) custom-call(f32[4]{0:T(128)} %wavelet_in.1, s32[1,16]{1,0:T(1,128)} %encoding_in.1, s32[1,16]{1,0:T(1,128)} %cells_in.1, s32[8,32]{1,0:T(8,128)} %depth_in.1, f32[1,4,8,32]{3,2,1,0:T(8,128)} %data_in.1, f32[1,9,8,32,128]{4,3,2,1,0:T(8,128)} %fwd_in.1, ...), custom_call_target="tpu_custom_call" | custom-call | tf_op jit(solution)/shard_map/pallas_call | solution.py:569
  56.6 1.5 %shard_map.104 = (f32[1,9,8,32,128]{4,3,2,1,0:T(8,128)}, f32[1,9,8,32,128]{4,3,2,1,0:T(8,128)}, f32[40,8,128]{2,1,0:T(8,128)}) custom-call(f32[2,9,10,48,128]{4,3,2,1,0:T(8,128)S(1)} %get-tuple-element.8.F, f32[40,8,128]{2,1,0:T(8,128)S(1)} %get-tuple-element.9.grad), custom_call_target="tpu_custom_call" | custom-call | tf_op jit(solution)/shard_map/pallas_call | solution.py:614
